TPU v7x, 128 devices: a whole 4x4x4 slice. The times are simulated.
128 devices in a mesh: row: 8 (over y, core), col: 16 (over z, x).
Axes of the slice: x: 4, y: 4, z: 4, core: 2. Of those that a mesh axis runs over, the one named last changes fastest.
Arguments:
- inputs: bfloat16 [1280, 6144], P('col', 'row'), may hold values from -6 to 6
- w_in: bfloat16 [6144, 24576], P('row', 'col'), may hold values from -0.078125 to 0.078125
- b_in: float32 [24576], P('col'), may hold values from -3 to 3
- w_out: bfloat16 [24576, 6144], P('col', 'row'), may hold values from -0.0390625 to 0.0390625
- b_out: float32 [6144], P('row'), may hold values from -3 to 3
- out_grad: bfloat16 [1280, 6144], P('col', 'row'), may hold values from -0.625 to 0.625
Outputs:
- output: bfloat16 [1280, 6144], P('col', 'row')
- input_grad: bfloat16 [1280, 6144], P('col', 'row')
- w_in_grad: float32 [6144, 24576], P('row', 'col')
- b_in_grad: float32 [24576], P('col')
- w_out_grad: float32 [24576, 6144], P('col', 'row')
- b_out_grad: float32 [6144], P('row')
All inputs are finite; a program needn't handle non-finite values.
Results may differ from a plain program's by a relative error of at most 0.007.
Values may be sent and summed in bfloat16 or wider, within the bound.
A program may use at most 128 MiB of HBM per device.

v0:
```python
import jax
import jax.numpy as jnp
from jax import lax
from jax.sharding import PartitionSpec as P


def gelu_parts(hidden):
    half = 0.5 * (1.0 + jax.scipy.special.erf(hidden * 0.7071067811865476))
    slope = half + hidden * jnp.exp(-0.5 * hidden * hidden) * 0.3989422804014327
    return (hidden * half, slope)


def shards(inputs, w_in, b_in, w_out, b_out, out_grad):
    inputs_all, grad_all = (
        lax.all_gather(inputs, "col", axis=0, tiled=True),
        lax.all_gather(out_grad, "col", axis=0, tiled=True),
    )
    partial_value = jnp.dot(inputs_all, w_in, preferred_element_type=jnp.float32)
    hidden = lax.psum(partial_value, "row") + b_in
    act, slope = gelu_parts(hidden)
    act_all = act.astype(jnp.bfloat16)
    rows = act_all
    output = (
        lax.psum_scatter(
            jnp.dot(rows, w_out, preferred_element_type=jnp.float32),
            "col",
            scatter_dimension=0,
            tiled=True,
        )
        + b_out
    ).astype(jnp.bfloat16)
    b_out_grad = jnp.sum(grad_all, axis=0, dtype=jnp.float32)
    w_out_grad = jnp.einsum("tf,td->fd", act_all, grad_all, preferred_element_type=jnp.float32)
    partial_grad = jnp.einsum("td,fd->tf", grad_all, w_out, preferred_element_type=jnp.float32)
    act_grad = lax.psum(partial_grad, "row")
    pre_grad = (act_grad * slope).astype(jnp.bfloat16)
    b_in_grad = jnp.sum(pre_grad, axis=0, dtype=jnp.float32)
    w_in_grad = jnp.einsum("td,tf->df", inputs_all, pre_grad, preferred_element_type=jnp.float32)
    rows = pre_grad
    input_grad = lax.psum_scatter(
        jnp.einsum("tf,df->td", rows, w_in, preferred_element_type=jnp.float32),
        "col",
        scatter_dimension=0,
        tiled=True,
    ).astype(jnp.bfloat16)
    return (output, input_grad, w_in_grad, b_in_grad, w_out_grad, b_out_grad)


def solution(mesh):
    placed = (
        P("col", "row"),
        P("row", "col"),
        P("col"),
        P("col", "row"),
        P("row"),
        P("col", "row"),
    )
    return jax.shard_map(
        shards,
        mesh=mesh,
        in_specs=placed,
        out_specs=(
            P("col", "row"),
            P("col", "row"),
            P("row", "col"),
            P("col"),
            P("col", "row"),
            P("row"),
        ),
        check_vma=False,
    )
```

profile of v0, /device:TPU:0, one launch (start us, length us, event | category | flops | bytes accessed | tf_op | source)
XLA Modules:
  0.0 465.8 jit_solution(393771307948937727)
XLA Ops:
  7.2 0.0 copy-start
  7.2 0.0 all-gather.5.cloned.1.call-start
  7.2 0.7 all-gather.5.cloned.1.call-update
  7.9 0.0 all-gather.3.cloned.1.call-start
  8.0 0.7 all-gather.3.cloned.1.call-update
  8.7 0.0 all-reduce.3.cloned.1.call-start
  8.7 48.7 %all-gather.5.cloned.1.call-done = bf16[1280,768]{1,0:T(8,128)(2,1)} async-done(((bf16[80,768]{1,0:T(8,128)(2,1)}), bf16[1280,768]{1,0:T(8,128)(2,1)}) %all-gather.5.cloned.1.call-update) | async-done | bytes 1966096 | tf_op jit(solution)/shard_map/all_gather | solution.py:16
  57.4 8.7 %fusion.9 = f32[1280,1536]{1,0:T(8,128)} fusion(bf16[1280,768]{1,0:T(8,128)(2,1)} %all-gather.5.cloned.1.call-done, bf16[1536,768]{1,0:T(8,128)(2,1)} %param.9), kind=kOutput, calls=%fused_computation.15 | convolution fusion | flops 3019898880 | bytes 12189696 | tf_op jit(solution)/shard_map/td,fd->tf/dot_general | solution.py:34
  66.1 37.5 %all-gather.3.cloned.1.call-done = bf16[1280,768]{1,0:T(8,128)(2,1)} async-done(((bf16[80,768]{1,0:T(8,128)(2,1)}), bf16[1280,768]{1,0:T(8,128)(2,1)}) %all-gather.3.cloned.1.call-update) | async-done | bytes 1966096 | tf_op jit(solution)/shard_map/all_gather | solution.py:15
  103.5 0.0 copy-done
  103.5 7.0 %fusion.7 = f32[1280,1536]{1,0:T(8,128)} fusion(bf16[1280,768]{1,0:T(8,128)(2,1)} %all-gather.3.cloned.1.call-done, bf16[768,1536]{1,0:T(8,128)(2,1)S(1)} %copy-done), kind=kOutput, calls=%fused_computation.13 | convolution fusion | flops 3019898880 | bytes 12189696 | tf_op jit(solution)/shard_map/dot_general | solution.py:18
  110.5 0.0 copy-start.4
  110.5 0.0 all-reduce.3.cloned.1.call-update
  110.5 0.0 reduce-scatter.5.cloned.1.call-start
  110.6 173.0 %all-reduce.3.cloned.1.call-done = (f32[1280,1536]{1,0:T(8,128)}, f32[1280,1536]{1,0:T(8,128)}) async-done(((f32[1280,1536]{1,0:T(8,128)}, f32[1280,1536]{1,0:T(8,128)}), (f32[1280,1536]{1,0:T(8,128)}, f32[1280,1536]{1,0:T(8,128)})) %all-reduce.3.cloned.1.call-update) | async-done | bytes 15728656 | tf_op jit(solution)/shard_map/psum | solution.py:19
  283.6 0.0 copy-done.4
  283.6 10.6 %convert_reduce_fusion = (f32[1536]{0:T(1024)}, bf16[1280,1536]{1,0:T(8,128)(2,1)S(1)}, bf16[1280,1536]{1,0:T(8,128)(2,1)}) fusion(f32[1280,1536]{1,0:T(8,128)} %get-tuple-element.13, f32[1280,1536]{1,0:T(8,128)} %get-tuple-element.12, f32[1536]{0:T(1024)S(1)} %copy-done.4), kind=kLoop, calls=%fused_computation.7 | loop fusion | flops 29489664 | bytes 23605248 | tf_op jit(solution)/shard_map/reduce_sum | solution.py:37
  294.2 0.0 copy-start.2
  294.2 1.9 copy-done.2
  296.1 5.1 %fusion.10 = f32[1280,768]{1,0:T(8,128)} fusion(bf16[1280,1536]{1,0:T(8,128)(2,1)S(1)} %get-tuple-element.15, bf16[768,1536]{1,0:T(8,128)(2,1)S(1)} %copy-done), kind=kOutput, calls=%fused_computation.16 | convolution fusion | flops 3019898880 | bytes 10223616 | tf_op jit(solution)/shard_map/tf,df->td/dot_general | solution.py:41
  301.2 0.0 copy-start.6
  301.2 0.0 reduce-scatter.5.cloned.1.call-update
  301.3 0.2 reduce-scatter.3.cloned.1.call-start
  301.5 1.4 copy-done.6
  302.9 7.2 %fusion.8 = f32[1280,768]{1,0:T(8,128)} fusion(bf16[1280,1536]{1,0:T(8,128)(2,1)} %get-tuple-element.16, bf16[1536,768]{1,0:T(8,128)(2,1)S(1)} %copy-done.6), kind=kOutput, calls=%fused_computation.14 | convolution fusion | flops 3019898880 | bytes 10223616 | tf_op jit(solution)/shard_map/dot_general | solution.py:25
  310.1 0.0 copy-start.3
  310.1 0.0 reduce-scatter.3.cloned.1.call-update
  310.1 1.6 copy-done.3
  311.7 0.9 convert_reduce_fusion.1
  312.6 8.2 %convolution_bitcast_fusion = f32[768,1536]{0,1:T(8,128)} fusion(bf16[1280,1536]{1,0:T(8,128)(2,1)} %copy-done.2, bf16[1280,768]{1,0:T(8,128)(2,1)} %all-gather.3.cloned.1.call-done), kind=kOutput, calls=%fused_computation.11 | convolution fusion | flops 3019898880 | bytes 10616832 | tf_op jit(solution)/shard_map/td,tf->df/dot_general | solution.py:38
  320.8 6.1 %copy.12 = f32[768,1536]{1,0:T(8,128)} copy(f32[768,1536]{0,1:T(8,128)} %convolution_bitcast_fusion) | data formatting | bytes 9437184
  327.0 0.0 copy-start.5
  327.0 0.0 copy-start.1
  327.0 8.4 %fusion.11 = f32[1536,768]{1,0:T(8,128)} fusion(bf16[1280,1536]{1,0:T(8,128)(2,1)} %get-tuple-element.16, bf16[1280,768]{1,0:T(8,128)(2,1)} %all-gather.5.cloned.1.call-done), kind=kOutput, calls=%fused_computation.17 | convolution fusion | flops 3019898880 | bytes 10616832 | tf_op jit(solution)/shard_map/tf,td->fd/dot_general | solution.py:33
  335.4 42.9 %reduce-scatter.5.cloned.1.call-done = f32[80,768]{1,0:T(8,128)} async-done(((f32[1280,768]{1,0:T(8,128)}), f32[80,768]{1,0:T(8,128)}) %reduce-scatter.5.cloned.1.call-update) | async-done | bytes 245776 | tf_op jit(solution)/shard_map/reduce_scatter | solution.py:40
  378.3 1.6 convert_element_type.21
  379.9 77.8 %reduce-scatter.3.cloned.1.call-done = f32[80,768]{1,0:T(8,128)} async-done(((f32[1280,768]{1,0:T(8,128)}), f32[80,768]{1,0:T(8,128)}) %reduce-scatter.3.cloned.1.call-update) | async-done | bytes 245776 | tf_op jit(solution)/shard_map/reduce_scatter | solution.py:24
  457.7 0.0 copy-done.5
  457.7 1.6 add_convert_fusion
  459.3 0.0 copy-done.1
Async XLA Ops:
  7.2 96.4 %copy-start = (bf16[768,1536]{1,0:T(8,128)(2,1)S(1)}, bf16[768,1536]{1,0:T(8,128)(2,1)}, u32[]{:S(2)}) copy-start(bf16[768,1536]{1,0:T(8,128)(2,1)} %param.7) | copy-start | bytes 7077892
  7.2 50.2 %all-gather.5.cloned.1.call-start = ((), (), s32[]{:S(2)}) async-start(), calls=%async_computation.4 | async-start | bytes 2088960 | tf_op jit(solution)/shard_map/all_gather | solution.py:16
  7.9 95.6 %all-gather.3.cloned.1.call-start = ((), (), s32[]{:S(2)}) async-start(), calls=%async_computation.2 | async-start | bytes 2088960 | tf_op jit(solution)/shard_map/all_gather | solution.py:15
  8.7 274.9 %all-reduce.3.cloned.1.call-start = ((), (), s32[]{:S(2)}) async-start(), calls=%async_computation.6 | async-start | bytes 31457280 | tf_op jit(solution)/shard_map/psum | solution.py:19
  110.5 173.1 %copy-start.4 = (f32[1536]{0:T(1024)S(1)}, f32[1536]{0:T(1024)}, u32[]{:S(2)}) copy-start(f32[1536]{0:T(1024)} %param.8) | copy-start | bytes 18436
  110.5 267.7 %reduce-scatter.5.cloned.1.call-start = ((), (), s32[]{:S(2)}) async-start(), calls=%async_computation.5 | async-start | bytes 4177920 | tf_op jit(solution)/shard_map/reduce_scatter | solution.py:40
  294.2 1.9 copy-start.2
  301.2 1.7 copy-start.6
  301.3 156.4 %reduce-scatter.3.cloned.1.call-start = ((), (), s32[]{:S(2)}) async-start(), calls=%async_computation.3 | async-start | bytes 4177920 | tf_op jit(solution)/shard_map/reduce_scatter | solution.py:24
  310.1 1.6 copy-start.3
  327.0 130.7 %copy-start.5 = (f32[768]{0:T(1024)S(1)}, f32[768]{0:T(1024)}, u32[]{:S(2)}) copy-start(f32[768]{0:T(1024)} %param.10) | copy-start | bytes 9220
  327.0 132.3 %copy-start.1 = (bf16[768,1536]{1,0:T(8,128)(2,1)S(1)}, bf16[768,1536]{1,0:T(8,128)(2,1)}, u32[]{:S(2)}) copy-start(bf16[768,1536]{1,0:T(8,128)(2,1)} %param.7) | copy-start | bytes 7077892
Sparse Core Ops, SparseCore 0:
  10.2 47.1 all-gather.4
  59.5 43.9 all-gather.2
  110.6 172.8 all-reduce.2
  301.4 76.8 reduce-scatter.4
  381.5 76.1 reduce-scatter.2
where the time goes:
time: 466 us
  waiting for transfers between devices  381 us (82%)
  matrix products  44.6 us (10%)
  other arithmetic  14.7 us (3%)
  between operations  13.8 us (3%)
  local copies, waits for them, and re-layouts  11 us (2%)
    psum x1, waiting for transfers between devices, shards(): hidden = lax.psum(partial_value, 'row') + b_in  173 us
    reduce_scatter x1, waiting for transfers between devices, shards(): lax.psum_scatter(jnp.dot(rows, w_out, preferred_element_type=jnp.float32)...  77.8 us
    all_gather x1, waiting for transfers between devices, shards(): lax.all_gather(out_grad, 'col', axis=0, tiled=True)  48.7 us
    reduce_scatter x1, waiting for transfers between devices, shards(): lax.psum_scatter(jnp.einsum('tf,df->td', rows, w_in, preferred_element_ty...  42.9 us
    all_gather x1, waiting for transfers between devices, shards(): lax.all_gather(inputs, 'col', axis=0, tiled=True)  37.5 us
    unnamed x15, local copies, waits for them, and re-layouts  11 us
    reduce_sum x1, other arithmetic, shards(): b_in_grad = jnp.sum(pre_grad, axis=0, dtype=jnp.float32)  10.6 us
  transfers between devices with their start and end apart: 5, of which 5 were waited for; matrix products, arithmetic and copies ran while one was open for 9% of the time, Pallas kernels for 0%

commit v1 on v0

--- a/solution.py
+++ b/solution.py
@@ -1,7 +1,22 @@
+import functools
 import jax
 import jax.numpy as jnp
 from jax import lax
 from jax.sharding import PartitionSpec as P
+
+
+def check_layers_all(x_part, mesh_dim, dim_i):
+    local_part = lax.axis_size(mesh_dim)
+    s_next = jnp.concatenate(
+        lax.all_to_all(
+            jnp.stack([x_part] * local_part, 0), axis_name=mesh_dim, split_axis=0, concat_axis=0
+        ),
+        dim_i,
+    )
+    return s_next
+
+
+outputs_unite = functools.partial(check_layers_all, mesh_dim="col", dim_i=0)
 
 
 def gelu_parts(hidden):
@@ -13,7 +28,7 @@
 def shards(inputs, w_in, b_in, w_out, b_out, out_grad):
     inputs_all, grad_all = (
         lax.all_gather(inputs, "col", axis=0, tiled=True),
-        lax.all_gather(out_grad, "col", axis=0, tiled=True),
+        outputs_unite(out_grad),
     )
     partial_value = jnp.dot(inputs_all, w_in, preferred_element_type=jnp.float32)
     hidden = lax.psum(partial_value, "row") + b_in

time: 466 us -> 429 us (0.921)
  waiting for transfers between devices: 381 us -> 308 us
  blocking collectives: 0 us -> 36.7 us
    all_gather x1 -> x0, waiting for transfers between devices: 48.7 us -> none  [shards(): lax.all_gather(out_grad, 'col', axis=0, tiled=True)]
    all_to_all x0 -> x1, blocking collectives: none -> 36.7 us  [check_layers_all(): lax.all_to_all(jnp.stack([x_part] * local_part, 0), axis_name=mesh_dim, s...]
    all_gather x1, waiting for transfers between devices: 37.5 us -> 13.1 us  [shards(): lax.all_gather(inputs, 'col', axis=0, tiled=True)]
    unnamed x15 -> x19, local copies, waits for them, and re-layouts: 11 us -> 12.3 us
  transfers between devices with their start and end apart: 5 -> 4, of which waited for: 5 -> 4; matrix products, arithmetic and copies ran while one was open for 9% -> 9% of each run, Pallas kernels for 0% -> 0%
where the time goes in v1:
time: 429 us; the launch traced here: 428 us
  waiting for transfers between devices  308 us (72%)
  matrix products  41.3 us (10%)
  blocking collectives  36.7 us (9%)
  other arithmetic  14.8 us (3%)
  between operations  13.8 us (3%)
  local copies, waits for them, and re-layouts  13.5 us (3%)
    psum x1, waiting for transfers between devices, shards(): hidden = lax.psum(partial_value, 'row') + b_in  173 us
    reduce_scatter x1, waiting for transfers between devices, shards(): lax.psum_scatter(jnp.dot(rows, w_out, preferred_element_type=jnp.float32)...  77.9 us
    reduce_scatter x1, waiting for transfers between devices, shards(): lax.psum_scatter(jnp.einsum('tf,df->td', rows, w_in, preferred_element_ty...  43 us
    all_to_all x1, blocking collectives, check_layers_all(): lax.all_to_all(jnp.stack([x_part] * local_part, 0), axis_name=mesh_dim, s...  36.7 us
    all_gather x1, waiting for transfers between devices, shards(): lax.all_gather(inputs, 'col', axis=0, tiled=True)  13.1 us
    unnamed x19, local copies, waits for them, and re-layouts  12.3 us
    reduce_sum x1, other arithmetic, shards(): b_in_grad = jnp.sum(pre_grad, axis=0, dtype=jnp.float32)  10.6 us
  transfers between devices with their start and end apart: 4, of which 4 were waited for; matrix products, arithmetic and copies ran while one was open for 9% of the time, Pallas kernels for 0%

profile of v1, /device:TPU:0, one launch (start us, length us, event | category | flops | bytes accessed | tf_op | source)
XLA Modules:
  0.0 428.1 jit_solution(4999324123319837089)
XLA Ops:
  7.2 0.0 copy-start
  7.2 0.0 all-gather.2.cloned.1.call-start
  7.2 0.7 all-gather.2.cloned.1.call-update
  7.9 0.0 all-reduce.3.cloned.1.call-start
  8.0 0.0 copy-start.7
  8.0 1.2 stack.2
  9.2 36.7 %all_to_all.5 = bf16[16,80,768]{2,1,0:T(8,128)(2,1)S(1)} all-to-all(bf16[16,80,768]{2,1,0:T(8,128)(2,1)S(1)} %stack.2), channel_id=1, replica_groups=mesh['row'=8,'col'=16] {'col'}, dimensions={0} | all-to-all | bytes 3932160 | tf_op jit(solution)/shard_map/all_to_all | solution.py:11
  45.9 0.0 copy-start.2
  45.9 1.3 copy-done.2
  47.1 0.0 copy-done.7
  47.1 5.4 %fusion.9 = f32[1280,1536]{1,0:T(8,128)} fusion(bf16[1280,768]{1,0:T(8,128)(2,1)S(1)} %bitcast.15, bf16[1536,768]{1,0:T(8,128)(2,1)S(1)} %copy-done.7), kind=kOutput, calls=%fused_computation.15 | convolution fusion | flops 3019898880 | bytes 12189696 | tf_op jit(solution)/shard_map/td,fd->tf/dot_general | solution.py:49
  52.5 13.1 %all-gather.2.cloned.1.call-done = bf16[1280,768]{1,0:T(8,128)(2,1)} async-done(((bf16[80,768]{1,0:T(8,128)(2,1)}), bf16[1280,768]{1,0:T(8,128)(2,1)}) %all-gather.2.cloned.1.call-update) | async-done | bytes 1966096 | tf_op jit(solution)/shard_map/all_gather | solution.py:30
  65.6 0.0 copy-done
  65.6 6.9 %fusion.7 = f32[1280,1536]{1,0:T(8,128)} fusion(bf16[1280,768]{1,0:T(8,128)(2,1)} %all-gather.2.cloned.1.call-done, bf16[768,1536]{1,0:T(8,128)(2,1)S(1)} %copy-done), kind=kOutput, calls=%fused_computation.13 | convolution fusion | flops 3019898880 | bytes 12189696 | tf_op jit(solution)/shard_map/dot_general | solution.py:33
  72.5 0.0 copy-start.5
  72.5 0.0 all-reduce.3.cloned.1.call-update
  72.6 0.0 reduce-scatter.5.cloned.1.call-start
  72.6 173.0 %all-reduce.3.cloned.1.call-done = (f32[1280,1536]{1,0:T(8,128)}, f32[1280,1536]{1,0:T(8,128)}) async-done(((f32[1280,1536]{1,0:T(8,128)}, f32[1280,1536]{1,0:T(8,128)}), (f32[1280,1536]{1,0:T(8,128)}, f32[1280,1536]{1,0:T(8,128)})) %all-reduce.3.cloned.1.call-update) | async-done | bytes 15728656 | tf_op jit(solution)/shard_map/psum | solution.py:34
  245.6 0.0 copy-done.5
  245.6 10.6 %convert_reduce_fusion = (f32[1536]{0:T(1024)}, bf16[1280,1536]{1,0:T(8,128)(2,1)S(1)}, bf16[1280,1536]{1,0:T(8,128)(2,1)}) fusion(f32[1280,1536]{1,0:T(8,128)} %get-tuple-element.19, f32[1280,1536]{1,0:T(8,128)} %get-tuple-element.18, f32[1536]{0:T(1024)S(1)} %copy-done.5), kind=kLoop, calls=%fused_computation.7 | loop fusion | flops 29489664 | bytes 23605248 | tf_op jit(solution)/shard_map/reduce_sum | solution.py:52
  256.3 0.0 copy-start.4
  256.3 1.9 copy-done.4
  258.2 5.1 %fusion.10 = f32[1280,768]{1,0:T(8,128)} fusion(bf16[1280,1536]{1,0:T(8,128)(2,1)S(1)} %get-tuple-element.21, bf16[768,1536]{1,0:T(8,128)(2,1)S(1)} %copy-done), kind=kOutput, calls=%fused_computation.16 | convolution fusion | flops 3019898880 | bytes 10223616 | tf_op jit(solution)/shard_map/tf,df->td/dot_general | solution.py:56
  263.3 0.0 copy-start.8
  263.3 0.0 reduce-scatter.5.cloned.1.call-update
  263.3 0.2 reduce-scatter.3.cloned.1.call-start
  263.6 1.4 copy-done.8
  265.0 7.2 %fusion.8 = f32[1280,768]{1,0:T(8,128)} fusion(bf16[1280,1536]{1,0:T(8,128)(2,1)} %get-tuple-element.22, bf16[1536,768]{1,0:T(8,128)(2,1)S(1)} %copy-done.8), kind=kOutput, calls=%fused_computation.14 | convolution fusion | flops 3019898880 | bytes 10223616 | tf_op jit(solution)/shard_map/dot_general | solution.py:40
  272.2 0.0 copy-start.3
  272.2 0.0 reduce-scatter.3.cloned.1.call-update
  272.2 1.6 copy-done.3
  273.8 0.9 convert_reduce_fusion.1
  274.7 8.2 %convolution_bitcast_fusion = f32[768,1536]{0,1:T(8,128)} fusion(bf16[1280,1536]{1,0:T(8,128)(2,1)} %copy-done.4, bf16[1280,768]{1,0:T(8,128)(2,1)} %all-gather.2.cloned.1.call-done), kind=kOutput, calls=%fused_computation.11 | convolution fusion | flops 3019898880 | bytes 10616832 | tf_op jit(solution)/shard_map/td,tf->df/dot_general | solution.py:53
  282.9 6.1 %copy.13 = f32[768,1536]{1,0:T(8,128)} copy(f32[768,1536]{0,1:T(8,128)} %convolution_bitcast_fusion) | data formatting | bytes 9437184
  289.0 0.0 copy-start.6
  289.0 0.0 copy-start.1
  289.0 8.4 %fusion.11 = f32[1536,768]{1,0:T(8,128)} fusion(bf16[1280,1536]{1,0:T(8,128)(2,1)} %get-tuple-element.22, bf16[1280,768]{1,0:T(8,128)(2,1)} %bitcast.16), kind=kOutput, calls=%fused_computation.17 | convolution fusion | flops 3019898880 | bytes 10616832 | tf_op jit(solution)/shard_map/tf,td->fd/dot_general | solution.py:48
  297.5 43.0 %reduce-scatter.5.cloned.1.call-done = f32[80,768]{1,0:T(8,128)} async-done(((f32[1280,768]{1,0:T(8,128)}), f32[80,768]{1,0:T(8,128)}) %reduce-scatter.5.cloned.1.call-update) | async-done | bytes 245776 | tf_op jit(solution)/shard_map/reduce_scatter | solution.py:55
  340.5 1.6 convert_element_type.22
  342.1 77.9 %reduce-scatter.3.cloned.1.call-done = f32[80,768]{1,0:T(8,128)} async-done(((f32[1280,768]{1,0:T(8,128)}), f32[80,768]{1,0:T(8,128)}) %reduce-scatter.3.cloned.1.call-update) | async-done | bytes 245776 | tf_op jit(solution)/shard_map/reduce_scatter | solution.py:39
  420.0 0.0 copy-done.6
  420.0 1.6 add_convert_fusion
  421.6 0.0 copy-done.1
Async XLA Ops:
  7.2 58.4 %copy-start = (bf16[768,1536]{1,0:T(8,128)(2,1)S(1)}, bf16[768,1536]{1,0:T(8,128)(2,1)}, u32[]{:S(2)}) copy-start(bf16[768,1536]{1,0:T(8,128)(2,1)} %param.7) | copy-start | bytes 7077892
  7.2 58.4 %all-gather.2.cloned.1.call-start = ((), (), s32[]{:S(2)}) async-start(), calls=%async_computation.3 | async-start | bytes 2088960 | tf_op jit(solution)/shard_map/all_gather | solution.py:30
  7.9 237.7 %all-reduce.3.cloned.1.call-start = ((), (), s32[]{:S(2)}) async-start(), calls=%async_computation.6 | async-start | bytes 31457280 | tf_op jit(solution)/shard_map/psum | solution.py:34
  8.0 39.2 %copy-start.7 = (bf16[1536,768]{1,0:T(8,128)(2,1)S(1)}, bf16[1536,768]{1,0:T(8,128)(2,1)}, u32[]{:S(2)}) copy-start(bf16[1536,768]{1,0:T(8,128)(2,1)} %param.9) | copy-start | bytes 7077892
  45.9 1.3 copy-start.2
  72.5 173.1 %copy-start.5 = (f32[1536]{0:T(1024)S(1)}, f32[1536]{0:T(1024)}, u32[]{:S(2)}) copy-start(f32[1536]{0:T(1024)} %param.8) | copy-start | bytes 18436
  72.6 267.9 %reduce-scatter.5.cloned.1.call-start = ((), (), s32[]{:S(2)}) async-start(), calls=%async_computation.5 | async-start | bytes 4177920 | tf_op jit(solution)/shard_map/reduce_scatter | solution.py:55
  256.3 1.9 copy-start.4
  263.3 1.7 copy-start.8
  263.3 156.6 %reduce-scatter.3.cloned.1.call-start = ((), (), s32[]{:S(2)}) async-start(), calls=%async_computation.4 | async-start | bytes 4177920 | tf_op jit(solution)/shard_map/reduce_scatter | solution.py:39
  272.2 1.6 copy-start.3
  289.0 130.9 %copy-start.6 = (f32[768]{0:T(1024)S(1)}, f32[768]{0:T(1024)}, u32[]{:S(2)}) copy-start(f32[768]{0:T(1024)} %param.10) | copy-start | bytes 9220
  289.0 132.5 %copy-start.1 = (bf16[768,1536]{1,0:T(8,128)(2,1)S(1)}, bf16[768,1536]{1,0:T(8,128)(2,1)}, u32[]{:S(2)}) copy-start(bf16[768,1536]{1,0:T(8,128)(2,1)} %param.7) | copy-start | bytes 7077892
Sparse Core Ops, SparseCore 0:
  10.2 55.3 all-gather.1
  72.7 172.8 all-reduce.2
  263.5 76.9 reduce-scatter.4
  343.7 76.2 reduce-scatter.2
